TPU v7x, 512 devices: a whole 4x8x8 slice. The times are simulated.
512 devices in a mesh: gx: 16 (over z, core), gy: 8 (over y), gz: 4 (over x).
Axes of the slice: x: 4, y: 8, z: 8, core: 2. Of those that a mesh axis runs over, the one named last changes fastest.
Arguments:
- start: float32 [4, 80, 256, 512], P(None, 'gx', 'gy', 'gz'), may hold values from -6 to 6
- rhs_block: float32 [4, 80, 256, 512], P(None, 'gx', 'gy', 'gz'), may hold values from -6 to 6
- coefficients: float32 [4, 80, 256, 512], P(None, 'gx', 'gy', 'gz'), may hold values from 0.5 to 2
Outputs:
- solution: float32 [4, 80, 256, 512], P(None, 'gx', 'gy', 'gz')
All inputs are finite; a program needn't handle non-finite values.
Results may differ from a plain program's by a relative error of at most 0.0003.
Values sent between devices are 32-bit elements; how exact they have to be, the bound alone decides.
A program may use at most 192 MiB of HBM per device.

v0:
```python
import jax
import jax.numpy as jnp
from jax import lax
from jax.sharding import PartitionSpec as P

S = 4
basis_shift = 8.75
basis_scale = 4.0


def padded(block, sides, width):
    for axis, dim in sides:
        count = lax.axis_size(axis)
        forward = [(i, i + 1) for i in range(count - 1)]
        backward = [(target, source) for source, target in forward]
        low = lax.ppermute(
            lax.slice_in_dim(block, block.shape[dim] - width, None, axis=dim), axis, forward
        )
        high = lax.ppermute(lax.slice_in_dim(block, 0, width, axis=dim), axis, backward)
        block = jnp.concatenate([low, block, high], axis=dim)
    return block


def stencil(field, coefs):
    center = field[:, 1:-1, 1:-1, 1:-1]
    result = coefs[0, 1:-1, 1:-1, 1:-1] * center
    result = result + coefs[1, 1:-1, 1:-1, 1:-1] * (center - field[:, 2:, 1:-1, 1:-1])
    result = result + coefs[1, :-2, 1:-1, 1:-1] * (center - field[:, :-2, 1:-1, 1:-1])
    result = result + coefs[2, 1:-1, 1:-1, 1:-1] * (center - field[:, 1:-1, 2:, 1:-1])
    result = result + coefs[2, 1:-1, :-2, 1:-1] * (center - field[:, 1:-1, :-2, 1:-1])
    result = result + coefs[3, 1:-1, 1:-1, 1:-1] * (center - field[:, 1:-1, 1:-1, 2:])
    result = result + coefs[3, 1:-1, 1:-1, :-2] * (center - field[:, 1:-1, 1:-1, :-2])
    return result


def reflect_rows(tall):
    count = tall.shape[0]
    entries = tall.shape[1]
    position = jnp.arange(entries)
    for j in range(count):
        column = jnp.where(position >= j, tall[j], 0.0)
        length = jnp.sqrt(jnp.sum(column * column))
        leading = tall[j, j]
        mirror = -jnp.where(leading >= 0, 1.0, -1.0) * length
        vector = column - mirror * (position == j).astype(jnp.float32)
        weight = jnp.sum(vector * vector)
        project = jnp.dot(tall, vector, precision=lax.Precision.HIGHEST) / weight
        tall = tall - 2.0 * project[:, None] * vector[None, :]
    factor = tall.T
    flip_sign = jnp.where(jnp.diagonal(factor) >= 0, 1.0, -1.0)
    return jnp.triu(factor * flip_sign[:, None])


def back_solve(triangle, values):
    count = triangle.shape[0]
    answer = [None] * count
    for i in reversed(range(count)):
        partial_sum = values[i]
        for j in range(i + 1, count):
            partial_sum = partial_sum - triangle[i, j] * answer[j]
        answer[i] = partial_sum / triangle[i, i]
    return jnp.stack(answer)


def least_squares(upper, nrhs):
    total = upper.shape[0]
    kept = total - nrhs
    rows = jnp.arange(total)[:, None]
    cols = jnp.arange(kept)[None, :]
    shifts = basis_shift * (rows == cols).astype(jnp.float32) + basis_scale * (
        rows == cols + nrhs
    ).astype(jnp.float32)
    mixed = jnp.dot(upper, shifts, precision=lax.Precision.HIGHEST)
    joined = jnp.concatenate([mixed, upper[:, :nrhs]], axis=1)
    reduced = reflect_rows(joined.T)
    return back_solve(reduced[:kept, :kept], reduced[:kept, kept:])


def local(start, rhs_block, coefficients):
    nrhs = start.shape[0]
    guess_ext, coef_ext = (
        padded(start, (("gx", 1), ("gy", 2), ("gz", 3)), 1),
        padded(coefficients, (("gx", 1), ("gy", 2), ("gz", 3)), 1),
    )
    blocks = [rhs_block - stencil(guess_ext, coef_ext)]
    for step in range(S):
        before = blocks[-1]
        widened = padded(before, (("gx", 1), ("gy", 2), ("gz", 3)), 1)
        blocks.append((stencil(widened, coef_ext) - basis_shift * before) / basis_scale)
    tall = jnp.stack(blocks).reshape(len(blocks) * nrhs, -1)
    local_gram = jnp.dot(tall, tall.T, precision=lax.Precision.HIGHEST)
    gram = lax.psum(local_gram, ("gx", "gy", "gz"))
    upper = jnp.linalg.cholesky(gram).T
    weights = least_squares(upper, nrhs)
    kept = tall.shape[0] - nrhs
    update = jnp.dot(weights.T, tall[:kept], precision=lax.Precision.HIGHEST)
    return start + update.reshape(start.shape)


def solution(mesh):
    placed = (P(None, "gx", "gy", "gz"), P(None, "gx", "gy", "gz"), P(None, "gx", "gy", "gz"))
    return jax.shard_map(
        local, mesh=mesh, in_specs=placed, out_specs=P(None, "gx", "gy", "gz"), check_vma=False
    )
```

profile of v0, /device:TPU:1, one launch (start us, length us, event | category | flops | bytes accessed | tf_op | source)
XLA Modules:
  0.0 541.6 jit_solution(3785583033890651326)
XLA Ops:
  0.9 5.5 %collective-permute-start.1 = (f32[4,1,32,128]{3,2,1,0:T(8,128)S(1)}, f32[4,1,32,128]{3,2,1,0:T(8,128)S(1)}, u32[]{:S(2)}, u32[]{:S(2)}) collective-permute-start(f32[4,1,32,128]{3,2,1,0:T(8,128)S(1)} %get-tuple-element.80), channel_id=1, source_target_pairs={{0,32},{32,64},{64,96},{96,128},{128,160},{160,192},{192,224},{224... | collective-permute-start | bytes 196616 | tf_op jit(solution)/shard_map/ppermute | solution.py:16
  6.5 4.7 collective-permute-start.4
  12.1 1.9 collective-permute-start.2
  14.0 2.4 collective-permute-start
  24.1 5.2 collective-permute-start.6
  31.2 2.0 copy.479
  33.2 1.9 copy.481
  36.0 3.1 collective-permute-start.9
  45.9 4.0 collective-permute-start.10
  50.8 2.4 fusion.42
  56.7 2.2 constant_dynamic-update-slice_fusion.9
  58.9 1.9 collective-permute-start.11
  60.8 5.3 collective-permute-start.12
  68.8 4.0 collective-permute-start.14
  78.9 4.0 collective-permute-start.16
  88.8 1.9 collective-permute-start.17
  90.7 6.2 %collective-permute-start.18 = (f32[4,1,32,128]{3,2,1,0:T(8,128)S(1)}, f32[4,1,32,128]{3,2,1,0:T(8,128)S(1)}, u32[]{:S(2)}, u32[]{:S(2)}) collective-permute-start(f32[4,1,32,128]{3,2,1,0:T(8,128)S(1)} %get-tuple-element.70), channel_id=1, source_target_pairs={{0,32},{32,64},{64,96},{96,128},{128,160},{160,192},{192,224},{224... | collective-permute-start | bytes 196616 | tf_op jit(solution)/shard_map/ppermute | solution.py:16
  99.6 4.5 collective-permute-start.20
  107.2 4.5 collective-permute-start.22
  117.3 5.6 %collective-permute-start.24 = (f32[4,1,32,128]{3,2,1,0:T(8,128)S(1)}, f32[4,1,32,128]{3,2,1,0:T(8,128)S(1)}, u32[]{:S(2)}, u32[]{:S(2)}) collective-permute-start(f32[4,1,32,128]{3,2,1,0:T(8,128)S(1)} %get-tuple-element.68), channel_id=1, source_target_pairs={{0,32},{32,64},{64,96},{96,128},{128,160},{160,192},{192,224},{224... | collective-permute-start | bytes 196616 | tf_op jit(solution)/shard_map/ppermute | solution.py:16
  125.5 4.5 collective-permute-start.26
  133.1 4.5 collective-permute-start.28
  139.3 1.9 collective-permute-start.29
  141.2 6.0 %collective-permute-start.30 = (f32[4,1,32,128]{3,2,1,0:T(8,128)S(1)}, f32[4,1,32,128]{3,2,1,0:T(8,128)S(1)}, u32[]{:S(2)}, u32[]{:S(2)}) collective-permute-start(f32[4,1,32,128]{3,2,1,0:T(8,128)S(1)} %get-tuple-element.62), channel_id=1, source_target_pairs={{0,32},{32,64},{64,96},{96,128},{128,160},{160,192},{192,224},{224... | collective-permute-start | bytes 196616 | tf_op jit(solution)/shard_map/ppermute | solution.py:16
  149.9 5.5 %collective-permute-start.32 = (f32[4,7,1,128]{3,0,2,1:T(4,128)S(1)}, f32[4,7,1,128]{3,0,2,1:T(4,128)S(1)}, u32[]{:S(2)}, u32[]{:S(2)}) collective-permute-start(f32[4,7,1,128]{3,0,2,1:T(4,128)S(1)} %copy.517), channel_id=1, source_target_pairs={{0,4},{4,8},{8,12},{12,16},{16,20},{20,24},{24,28},{1,5},{5,9},{9,... | collective-permute-start | bytes 43016 | tf_op jit(solution)/shard_map/ppermute | solution.py:16
  159.0 5.1 collective-permute-start.34
  171.2 2.2 fusion.49
  175.2 2.1 fusion.311
  177.3 116.5 %psum.7 = f32[20,20]{0,1:T(8,128)S(1)} all-reduce(f32[20,20]{0,1:T(8,128)S(1)} %fusion.311), channel_id=1, replica_groups=mesh['gx'=16,'gy'=8,'gz'=4] {'gx','gy','gz'}, use_global_device_ids=true, to_apply=%region_0.0 | all-reduce | flops 400 | bytes 3200 | tf_op jit(solution)/shard_map/psum | solution.py:92
  395.1 65.5 %subtract_divide_fusion = (f32[1,4]{1,0:T(1,128)S(1)}, f32[1,4]{1,0:T(1,128)S(1)}, f32[1,4]{1,0:T(1,128)S(1)}, f32[1,4]{1,0:T(1,128)S(1)}, f32[1,4]{1,0:T(1,128)...) fusion(f32[20,20]{1,0:T(8,128)S(1)} %multiply_select_fusion, ...), kind=kLoop, calls=%fused_computation.602 | loop fusion | flops 784 | bytes 884 | tf_op jit(solution)/shard_map/div | solution.py:61
  461.0 57.8 %fusion.191 = (f32[4]{0:T(128)S(1)}, f32[4]{0:T(128)S(1)}, f32[4]{0:T(128)S(1)}, f32[4]{0:T(128)S(1)}, f32[4]{0:T(128)S(1)}, /*index=5*/f32[4]{0:T(128)S(1)}, f3...) fusion(f32[20,20]{1,0:T(8,128)S(1)} %multiply_select_fusion, f32[1,4]{1,0:T(1,128)S(1)} %get-tuple-element.16, ...), kind=kLoop, calls=%fused_computation.504 | loop fusion | flops 704 | bytes 756 | tf_op jit(solution)/shard_map/div | solution.py:61
  518.8 19.3 %fusion.244 = (f32[1,4]{1,0:T(1,128)S(1)}, f32[4]{0:T(128)S(1)}) fusion(f32[1,4]{1,0:T(1,128)S(1)} %get-tuple-element.19, f32[1,4]{1,0:T(1,128)S(1)} %get-tuple-element.18, f32[1,4]{1,0:T(1,128)S(1)} %get-tuple-element.17, f32[1,4]{1,0:T(1,128)S(1)} %get-tuple-element.16, f32[4]{0:T(128)S(1)} %get-tuple-element.31, f32[4]{0:T(128)S(1)} %get-tuple-element.30, ...), kind=kLoop, calls=%fused_computation.656 | loop fusion | flops 240 | bytes 412 | tf_op jit(solution)/shard_map/stack | solution.py:62
  (370 shorter events, 147.8 us)
Async XLA Ops:
  0.9 15.5 %collective-permute-start.1 = (f32[4,1,32,128]{3,2,1,0:T(8,128)S(1)}, f32[4,1,32,128]{3,2,1,0:T(8,128)S(1)}, u32[]{:S(2)}, u32[]{:S(2)}) collective-permute-start(f32[4,1,32,128]{3,2,1,0:T(8,128)S(1)} %get-tuple-element.80), channel_id=1, source_target_pairs={{0,32},{32,64},{64,96},{96,128},{128,160},{160,192},{192,224},{224... | collective-permute-start | bytes 196616 | tf_op jit(solution)/shard_map/ppermute | solution.py:16
  6.5 11.0 %collective-permute-start.4 = (f32[4,1,32,128]{3,2,1,0:T(8,128)S(1)}, f32[4,1,32,128]{3,2,1,0:T(8,128)S(1)}, u32[]{:S(2)}, u32[]{:S(2)}) collective-permute-start(f32[4,1,32,128]{3,2,1,0:T(8,128)S(1)} %get-tuple-element.79), channel_id=1, source_target_pairs={{32,0},{64,32},{96,64},{128,96},{160,128},{192,160},{224,192},{256... | collective-permute-start | bytes 196616 | tf_op jit(solution)/shard_map/ppermute | solution.py:19
  12.1 9.3 %collective-permute-start.2 = (f32[4,1,32,128]{3,2,1,0:T(8,128)S(1)}, f32[4,1,32,128]{3,2,1,0:T(8,128)S(1)}, u32[]{:S(2)}, u32[]{:S(2)}) collective-permute-start(f32[4,1,32,128]{3,2,1,0:T(8,128)S(1)} %get-tuple-element.82), channel_id=1, source_target_pairs={{0,32},{32,64},{64,96},{96,128},{128,160},{160,192},{192,224},{224... | collective-permute-start | bytes 196616 | tf_op jit(solution)/shard_map/ppermute | solution.py:16
  14.0 7.5 %collective-permute-start = (f32[4,1,32,128]{3,2,1,0:T(8,128)S(1)}, f32[4,1,32,128]{3,2,1,0:T(8,128)S(1)}, u32[]{:S(2)}, u32[]{:S(2)}) collective-permute-start(f32[4,1,32,128]{3,2,1,0:T(8,128)S(1)} %get-tuple-element.81), channel_id=1, source_target_pairs={{32,0},{64,32},{96,64},{128,96},{160,128},{192,160},{224,192},{256... | collective-permute-start | bytes 196616 | tf_op jit(solution)/shard_map/ppermute | solution.py:19
  18.4 12.8 %collective-permute-start.5 = (f32[4,7,1,128]{3,1,2,0:T(8,128)}, f32[4,7,1,128]{3,1,2,0:T(8,128)S(1)}, u32[]{:S(2)}, u32[]{:S(2)}) collective-permute-start(f32[4,7,1,128]{3,1,2,0:T(8,128)} %get-tuple-element.50), channel_id=1, source_target_pairs={{0,4},{4,8},{8,12},{12,16},{16,20},{20,24},{24,28},{1,5},{5,9},{9,... | collective-permute-start | bytes 43016 | tf_op jit(solution)/shard_map/ppermute | solution.py:16
  20.1 13.1 %collective-permute-start.8 = (f32[4,7,1,128]{3,1,2,0:T(8,128)}, f32[4,7,1,128]{3,1,2,0:T(8,128)S(1)}, u32[]{:S(2)}, u32[]{:S(2)}) collective-permute-start(f32[4,7,1,128]{3,1,2,0:T(8,128)} %get-tuple-element.51), channel_id=1, source_target_pairs={{4,0},{8,4},{12,8},{16,12},{20,16},{24,20},{28,24},{5,1},{9,5},{13... | collective-permute-start | bytes 43016 | tf_op jit(solution)/shard_map/ppermute | solution.py:19
  22.2 16.9 %collective-permute-start.3 = (f32[4,7,1,128]{3,0,2,1:T(4,128)}, f32[4,7,1,128]{3,0,2,1:T(4,128)}, u32[]{:S(2)}, u32[]{:S(2)}) collective-permute-start(f32[4,7,1,128]{3,0,2,1:T(4,128)} %copy.550), channel_id=1, source_target_pairs={{4,0},{8,4},{12,8},{16,12},{20,16},{24,20},{28,24},{5,1},{9,5},{13... | collective-permute-start | bytes 43016 | tf_op jit(solution)/shard_map/ppermute | solution.py:19
  24.1 15.8 %collective-permute-start.6 = (f32[4,7,1,128]{3,0,2,1:T(4,128)}, f32[4,7,1,128]{3,0,2,1:T(4,128)}, u32[]{:S(2)}, u32[]{:S(2)}) collective-permute-start(f32[4,7,1,128]{3,0,2,1:T(4,128)} %copy.551), channel_id=1, source_target_pairs={{0,4},{4,8},{8,12},{12,16},{16,20},{20,24},{24,28},{1,5},{5,9},{9,... | collective-permute-start | bytes 43016 | tf_op jit(solution)/shard_map/ppermute | solution.py:16
  36.0 14.8 %collective-permute-start.9 = (f32[4,7,34,1]{2,1,3,0:T(8,128)S(1)}, f32[4,7,34,1]{2,1,3,0:T(8,128)S(1)}, u32[]{:S(2)}, u32[]{:S(2)}) collective-permute-start(f32[4,7,34,1]{2,1,3,0:T(8,128)S(1)} %pad_maximum_fusion.93), channel_id=1, source_target_pairs={{0,1},{1,2},{2,3},{4,5},{5,6},{6,7},{8,9},{9,10},{10,11},{12,13},{... | collective-permute-start | bytes 11432 | tf_op jit(solution)/shard_map/ppermute | solution.py:16
  43.2 11.2 %collective-permute-start.7 = (f32[4,7,34,1]{2,0,3,1:T(4,128)S(1)}, f32[4,7,34,1]{2,0,3,1:T(4,128)S(1)}, u32[]{:S(2)}, u32[]{:S(2)}) collective-permute-start(f32[4,7,34,1]{2,0,3,1:T(4,128)S(1)} %copy.476), channel_id=1, source_target_pairs={{1,0},{2,1},{3,2},{5,4},{6,5},{7,6},{9,8},{10,9},{11,10},{13,12},{... | collective-permute-start | bytes 11432 | tf_op jit(solution)/shard_map/ppermute | solution.py:19
  45.9 9.7 %collective-permute-start.10 = (f32[4,7,34,1]{2,0,3,1:T(4,128)S(1)}, f32[4,7,34,1]{2,0,3,1:T(4,128)S(1)}, u32[]{:S(2)}, u32[]{:S(2)}) collective-permute-start(f32[4,7,34,1]{2,0,3,1:T(4,128)S(1)} %copy.483), channel_id=1, source_target_pairs={{0,1},{1,2},{2,3},{4,5},{5,6},{6,7},{8,9},{9,10},{10,11},{12,13},{... | collective-permute-start | bytes 11432 | tf_op jit(solution)/shard_map/ppermute | solution.py:16
  58.9 7.3 %collective-permute-start.11 = (f32[4,1,32,128]{3,2,1,0:T(8,128)S(1)}, f32[4,1,32,128]{3,2,1,0:T(8,128)S(1)}, u32[]{:S(2)}, u32[]{:S(2)}) collective-permute-start(f32[4,1,32,128]{3,2,1,0:T(8,128)S(1)} %get-tuple-element.73), channel_id=1, source_target_pairs={{32,0},{64,32},{96,64},{128,96},{160,128},{192,160},{224,192},{256... | collective-permute-start | bytes 196616 | tf_op jit(solution)/shard_map/ppermute | solution.py:19
  60.8 6.6 %collective-permute-start.12 = (f32[4,1,32,128]{3,2,1,0:T(8,128)S(1)}, f32[4,1,32,128]{3,2,1,0:T(8,128)S(1)}, u32[]{:S(2)}, u32[]{:S(2)}) collective-permute-start(f32[4,1,32,128]{3,2,1,0:T(8,128)S(1)} %get-tuple-element.72), channel_id=1, source_target_pairs={{0,32},{32,64},{64,96},{96,128},{128,160},{160,192},{192,224},{224... | collective-permute-start | bytes 196616 | tf_op jit(solution)/shard_map/ppermute | solution.py:16
  76.2 6.6 %collective-permute-start.15 = (f32[4,7,34,1]{2,0,3,1:T(4,128)S(1)}, f32[4,7,34,1]{2,0,3,1:T(4,128)S(1)}, u32[]{:S(2)}, u32[]{:S(2)}) collective-permute-start(f32[4,7,34,1]{2,0,3,1:T(4,128)S(1)} %copy.491), channel_id=1, source_target_pairs={{1,0},{2,1},{3,2},{5,4},{6,5},{7,6},{9,8},{10,9},{11,10},{13,12},{... | collective-permute-start | bytes 11432 | tf_op jit(solution)/shard_map/ppermute | solution.py:19
  88.8 8.2 %collective-permute-start.17 = (f32[4,1,32,128]{3,2,1,0:T(8,128)S(1)}, f32[4,1,32,128]{3,2,1,0:T(8,128)S(1)}, u32[]{:S(2)}, u32[]{:S(2)}) collective-permute-start(f32[4,1,32,128]{3,2,1,0:T(8,128)S(1)} %get-tuple-element.71), channel_id=1, source_target_pairs={{32,0},{64,32},{96,64},{128,96},{160,128},{192,160},{224,192},{256... | collective-permute-start | bytes 196616 | tf_op jit(solution)/shard_map/ppermute | solution.py:19
  90.7 7.5 %collective-permute-start.18 = (f32[4,1,32,128]{3,2,1,0:T(8,128)S(1)}, f32[4,1,32,128]{3,2,1,0:T(8,128)S(1)}, u32[]{:S(2)}, u32[]{:S(2)}) collective-permute-start(f32[4,1,32,128]{3,2,1,0:T(8,128)S(1)} %get-tuple-element.70), channel_id=1, source_target_pairs={{0,32},{32,64},{64,96},{96,128},{128,160},{160,192},{192,224},{224... | collective-permute-start | bytes 196616 | tf_op jit(solution)/shard_map/ppermute | solution.py:16
  98.3 5.9 %collective-permute-start.19 = (f32[4,7,1,128]{3,0,2,1:T(4,128)S(1)}, f32[4,7,1,128]{3,0,2,1:T(4,128)S(1)}, u32[]{:S(2)}, u32[]{:S(2)}) collective-permute-start(f32[4,7,1,128]{3,0,2,1:T(4,128)S(1)} %copy.495), channel_id=1, source_target_pairs={{4,0},{8,4},{12,8},{16,12},{20,16},{24,20},{28,24},{5,1},{9,5},{13... | collective-permute-start | bytes 43016 | tf_op jit(solution)/shard_map/ppermute | solution.py:19
  99.6 5.4 collective-permute-start.20
  105.6 7.0 %collective-permute-start.21 = (f32[4,7,34,1]{2,0,3,1:T(4,128)S(1)}, f32[4,7,34,1]{2,0,3,1:T(4,128)S(1)}, u32[]{:S(2)}, u32[]{:S(2)}) collective-permute-start(f32[4,7,34,1]{2,0,3,1:T(4,128)S(1)} %copy.501), channel_id=1, source_target_pairs={{1,0},{2,1},{3,2},{5,4},{6,5},{7,6},{9,8},{10,9},{11,10},{13,12},{... | collective-permute-start | bytes 11432 | tf_op jit(solution)/shard_map/ppermute | solution.py:19
  107.2 5.8 %collective-permute-start.22 = (f32[4,7,34,1]{2,0,3,1:T(4,128)S(1)}, f32[4,7,34,1]{2,0,3,1:T(4,128)S(1)}, u32[]{:S(2)}, u32[]{:S(2)}) collective-permute-start(f32[4,7,34,1]{2,0,3,1:T(4,128)S(1)} %copy.503), channel_id=1, source_target_pairs={{0,1},{1,2},{2,3},{4,5},{5,6},{6,7},{8,9},{9,10},{10,11},{12,13},{... | collective-permute-start | bytes 11432 | tf_op jit(solution)/shard_map/ppermute | solution.py:16
  115.3 7.5 %collective-permute-start.23 = (f32[4,1,32,128]{3,2,1,0:T(8,128)S(1)}, f32[4,1,32,128]{3,2,1,0:T(8,128)S(1)}, u32[]{:S(2)}, u32[]{:S(2)}) collective-permute-start(f32[4,1,32,128]{3,2,1,0:T(8,128)S(1)} %get-tuple-element.69), channel_id=1, source_target_pairs={{32,0},{64,32},{96,64},{128,96},{160,128},{192,160},{224,192},{256... | collective-permute-start | bytes 196616 | tf_op jit(solution)/shard_map/ppermute | solution.py:19
  117.3 6.9 %collective-permute-start.24 = (f32[4,1,32,128]{3,2,1,0:T(8,128)S(1)}, f32[4,1,32,128]{3,2,1,0:T(8,128)S(1)}, u32[]{:S(2)}, u32[]{:S(2)}) collective-permute-start(f32[4,1,32,128]{3,2,1,0:T(8,128)S(1)} %get-tuple-element.68), channel_id=1, source_target_pairs={{0,32},{32,64},{64,96},{96,128},{128,160},{160,192},{192,224},{224... | collective-permute-start | bytes 196616 | tf_op jit(solution)/shard_map/ppermute | solution.py:16
  124.2 5.9 %collective-permute-start.25 = (f32[4,7,1,128]{3,0,2,1:T(4,128)S(1)}, f32[4,7,1,128]{3,0,2,1:T(4,128)S(1)}, u32[]{:S(2)}, u32[]{:S(2)}) collective-permute-start(f32[4,7,1,128]{3,0,2,1:T(4,128)S(1)} %copy.505), channel_id=1, source_target_pairs={{4,0},{8,4},{12,8},{16,12},{20,16},{24,20},{28,24},{5,1},{9,5},{13... | collective-permute-start | bytes 43016 | tf_op jit(solution)/shard_map/ppermute | solution.py:19
  125.5 5.4 collective-permute-start.26
  131.5 6.1 %collective-permute-start.27 = (f32[4,7,34,1]{2,0,3,1:T(4,128)S(1)}, f32[4,7,34,1]{2,0,3,1:T(4,128)S(1)}, u32[]{:S(2)}, u32[]{:S(2)}) collective-permute-start(f32[4,7,34,1]{2,0,3,1:T(4,128)S(1)} %copy.511), channel_id=1, source_target_pairs={{1,0},{2,1},{3,2},{5,4},{6,5},{7,6},{9,8},{10,9},{11,10},{13,12},{... | collective-permute-start | bytes 11432 | tf_op jit(solution)/shard_map/ppermute | solution.py:19
  133.1 5.4 collective-permute-start.28
  139.3 7.9 %collective-permute-start.29 = (f32[4,1,32,128]{3,2,1,0:T(8,128)S(1)}, f32[4,1,32,128]{3,2,1,0:T(8,128)S(1)}, u32[]{:S(2)}, u32[]{:S(2)}) collective-permute-start(f32[4,1,32,128]{3,2,1,0:T(8,128)S(1)} %get-tuple-element.63), channel_id=1, source_target_pairs={{32,0},{64,32},{96,64},{128,96},{160,128},{192,160},{224,192},{256... | collective-permute-start | bytes 196616 | tf_op jit(solution)/shard_map/ppermute | solution.py:19
  141.2 7.3 %collective-permute-start.30 = (f32[4,1,32,128]{3,2,1,0:T(8,128)S(1)}, f32[4,1,32,128]{3,2,1,0:T(8,128)S(1)}, u32[]{:S(2)}, u32[]{:S(2)}) collective-permute-start(f32[4,1,32,128]{3,2,1,0:T(8,128)S(1)} %get-tuple-element.62), channel_id=1, source_target_pairs={{0,32},{32,64},{64,96},{96,128},{128,160},{160,192},{192,224},{224... | collective-permute-start | bytes 196616 | tf_op jit(solution)/shard_map/ppermute | solution.py:16
  148.6 7.5 %collective-permute-start.31 = (f32[4,7,1,128]{3,0,2,1:T(4,128)S(1)}, f32[4,7,1,128]{3,0,2,1:T(4,128)S(1)}, u32[]{:S(2)}, u32[]{:S(2)}) collective-permute-start(f32[4,7,1,128]{3,0,2,1:T(4,128)S(1)} %copy.515), channel_id=1, source_target_pairs={{4,0},{8,4},{12,8},{16,12},{20,16},{24,20},{28,24},{5,1},{9,5},{13... | collective-permute-start | bytes 43016 | tf_op jit(solution)/shard_map/ppermute | solution.py:19
  149.9 6.3 %collective-permute-start.32 = (f32[4,7,1,128]{3,0,2,1:T(4,128)S(1)}, f32[4,7,1,128]{3,0,2,1:T(4,128)S(1)}, u32[]{:S(2)}, u32[]{:S(2)}) collective-permute-start(f32[4,7,1,128]{3,0,2,1:T(4,128)S(1)} %copy.517), channel_id=1, source_target_pairs={{0,4},{4,8},{8,12},{12,16},{16,20},{20,24},{24,28},{1,5},{5,9},{9,... | collective-permute-start | bytes 43016 | tf_op jit(solution)/shard_map/ppermute | solution.py:16
  156.8 11.5 %collective-permute-start.33 = (f32[4,7,34,1]{2,0,3,1:T(4,128)S(1)}, f32[4,7,34,1]{2,0,3,1:T(4,128)}, u32[]{:S(2)}, u32[]{:S(2)}) collective-permute-start(f32[4,7,34,1]{2,0,3,1:T(4,128)S(1)} %copy.521), channel_id=1, source_target_pairs={{1,0},{2,1},{3,2},{5,4},{6,5},{7,6},{9,8},{10,9},{11,10},{13,12},{... | collective-permute-start | bytes 11432 | tf_op jit(solution)/shard_map/ppermute | solution.py:19
  159.0 10.4 %collective-permute-start.34 = (f32[4,7,34,1]{2,0,3,1:T(4,128)}, f32[4,7,34,1]{2,0,3,1:T(4,128)}, u32[]{:S(2)}, u32[]{:S(2)}) collective-permute-start(f32[4,7,34,1]{2,0,3,1:T(4,128)} %copy.523), channel_id=1, source_target_pairs={{0,1},{1,2},{2,3},{4,5},{5,6},{6,7},{8,9},{9,10},{10,11},{12,13},{... | collective-permute-start | bytes 11432 | tf_op jit(solution)/shard_map/ppermute | solution.py:16
  (29 other events, 672.9 us)
where the time goes:
time: 546 us; the launch traced here: 542 us
  other arithmetic  195 us (36%)
  blocking collectives  116 us (21%)
  starting transfers between devices  110 us (20%)
  local copies, waits for them, and re-layouts  62.4 us (11%)
  between operations  29.3 us (5%)
  matrix products  20.1 us (4%)
  waiting for transfers between devices  8.15 us (1%)
    div x2, other arithmetic, back_solve(): answer[i] = partial_sum / triangle[i, i]  123 us
    psum x1, blocking collectives, local(): gram = lax.psum(local_gram, ('gx', 'gy', 'gz'))  116 us
    ppermute x18, starting transfers between devices, padded(): lax.ppermute(lax.slice_in_dim(block, block.shape[dim] - width, None, axis...  81.2 us
    ppermute x17, starting transfers between devices, padded(): lax.ppermute(lax.slice_in_dim(block, 0, width, axis=dim), axis, backward)  28.9 us
    another operation x1, other arithmetic, back_solve(): return jnp.stack(answer)  19.3 us
    dot_general x20, matrix products, reflect_rows(): project = jnp.dot(tall, vector, precision=lax.Precision.HIGHEST) / weight  15.7 us
    reduce_sum x20, other arithmetic, reflect_rows(): length = jnp.sqrt(jnp.sum(column * column))  13.6 us
    reduce_sum x20, other arithmetic, reflect_rows(): weight = jnp.sum(vector * vector)  12 us
  transfers between devices with their start and end apart: 35, of which 8 were waited for; matrix products, arithmetic and copies ran while one was open for 6% of the time, Pallas kernels for 0%

commit v1 on v0

--- a/solution.py
+++ b/solution.py
@@ -89,7 +89,8 @@
         blocks.append((stencil(widened, coef_ext) - basis_shift * before) / basis_scale)
     tall = jnp.stack(blocks).reshape(len(blocks) * nrhs, -1)
     local_gram = jnp.dot(tall, tall.T, precision=lax.Precision.HIGHEST)
-    gram = lax.psum(local_gram, ("gx", "gy", "gz"))
+    pieces = lax.all_gather(local_gram, ("gx", "gy", "gz"), axis=0, tiled=False)
+    gram = pieces.sum(axis=0)
     upper = jnp.linalg.cholesky(gram).T
     weights = least_squares(upper, nrhs)
     kept = tall.shape[0] - nrhs

time: 546 us -> 596 us (1.092)
  blocking collectives: 116 us -> 168 us
  local copies, waits for them, and re-layouts: 62.4 us -> 53.7 us
    all_gather x0 -> x1, blocking collectives: none -> 168 us  [local(): pieces = lax.all_gather(local_gram, ('gx', 'gy', 'gz'), axis=0, tiled=False)]
    psum x1 -> x0, blocking collectives: 116 us -> none  [local(): gram = lax.psum(local_gram, ('gx', 'gy', 'gz'))]
  transfers between devices with their start and end apart: 35 -> 35, of which waited for: 8 -> 9; matrix products, arithmetic and copies ran while one was open for 6% -> 5% of each run, Pallas kernels for 0% -> 0%
where the time goes in v1:
time: 596 us; the launch traced here: 589 us
  other arithmetic  198 us (33%)
  blocking collectives  168 us (28%)
  starting transfers between devices  112 us (19%)
  local copies, waits for them, and re-layouts  53.7 us (9%)
  between operations  29.4 us (5%)
  matrix products  20.1 us (3%)
  waiting for transfers between devices  8.13 us (1%)
    all_gather x1, blocking collectives, local(): pieces = lax.all_gather(local_gram, ('gx', 'gy', 'gz'), axis=0, tiled=False)  168 us
    div x2, other arithmetic, back_solve(): answer[i] = partial_sum / triangle[i, i]  123 us
    ppermute x18, starting transfers between devices, padded(): lax.ppermute(lax.slice_in_dim(block, block.shape[dim] - width, None, axis...  82.7 us
    ppermute x17, starting transfers between devices, padded(): lax.ppermute(lax.slice_in_dim(block, 0, width, axis=dim), axis, backward)  28.9 us
    another operation x1, other arithmetic, back_solve(): return jnp.stack(answer)  19.3 us
    dot_general x20, matrix products, reflect_rows(): project = jnp.dot(tall, vector, precision=lax.Precision.HIGHEST) / weight  15.7 us
    reduce_sum x20, other arithmetic, reflect_rows(): length = jnp.sqrt(jnp.sum(column * column))  13.6 us
    reduce_sum x20, other arithmetic, reflect_rows(): weight = jnp.sum(vector * vector)  12 us
  transfers between devices with their start and end apart: 35, of which 9 were waited for; matrix products, arithmetic and copies ran while one was open for 5% of the time, Pallas kernels for 0%

profile of v1, /device:TPU:1, one launch (start us, length us, event | category | flops | bytes accessed | tf_op | source)
XLA Modules:
  0.0 588.7 jit_solution(14118948354361758518)
XLA Ops:
  0.9 5.5 collective-permute-start.1
  6.5 4.7 collective-permute-start.4
  12.1 1.9 collective-permute-start.2
  14.0 2.4 collective-permute-start
  22.2 4.6 collective-permute-start.6
  28.8 1.9 copy.472
  30.7 2.0 copy.474
  34.2 3.7 collective-permute-start.9
  43.2 4.6 collective-permute-start.10
  51.9 2.0 constant_dynamic-update-slice_fusion.9
  53.9 1.9 collective-permute-start.11
  55.9 5.3 collective-permute-start.12
  63.9 4.3 collective-permute-start.14
  71.2 4.0 collective-permute-start.16
  78.3 1.9 collective-permute-start.17
  80.3 6.3 %collective-permute-start.18 = (f32[4,1,32,128]{3,2,1,0:T(8,128)S(1)}, f32[4,1,32,128]{3,2,1,0:T(8,128)S(1)}, u32[]{:S(2)}, u32[]{:S(2)}) collective-permute-start(f32[4,1,32,128]{3,2,1,0:T(8,128)S(1)} %get-tuple-element.70), channel_id=1, source_target_pairs={{0,32},{32,64},{64,96},{96,128},{128,160},{160,192},{192,224},{224... | collective-permute-start | bytes 196616 | tf_op jit(solution)/shard_map/ppermute | solution.py:16
  89.2 4.5 collective-permute-start.20
  96.8 4.5 collective-permute-start.22
  105.0 1.9 collective-permute-start.23
  106.9 5.6 collective-permute-start.24
  115.1 5.1 collective-permute-start.26
  125.1 4.5 collective-permute-start.28
  133.3 6.0 %collective-permute-start.30 = (f32[4,1,32,128]{3,2,1,0:T(8,128)S(1)}, f32[4,1,32,128]{3,2,1,0:T(8,128)S(1)}, u32[]{:S(2)}, u32[]{:S(2)}) collective-permute-start(f32[4,1,32,128]{3,2,1,0:T(8,128)S(1)} %get-tuple-element.62), channel_id=1, source_target_pairs={{0,32},{32,64},{64,96},{96,128},{128,160},{160,192},{192,224},{224... | collective-permute-start | bytes 196616 | tf_op jit(solution)/shard_map/ppermute | solution.py:16
  141.9 5.5 collective-permute-start.32
  151.6 5.1 collective-permute-start.34
  163.8 2.3 fusion.49
  167.8 2.1 convolution_bitcast_fusion
  170.0 167.6 %all-gather.1 = f32[512,20,20]{2,1,0:T(8,128)} all-gather(f32[1,20,20]{2,1,0:T(8,128)S(1)} %convolution_bitcast_fusion), channel_id=2, replica_groups=mesh['gx'=16,'gy'=8,'gz'=4] {'gx','gy','gz'}, dimensions={0}, use_global_device_ids=true | all-gather | bytes 820800 | tf_op jit(solution)/shard_map/all_gather | solution.py:92
  337.5 3.4 reduce_sum.369
  442.2 65.5 %subtract_divide_fusion = (f32[1,4]{1,0:T(1,128)S(1)}, f32[1,4]{1,0:T(1,128)S(1)}, f32[1,4]{1,0:T(1,128)S(1)}, f32[1,4]{1,0:T(1,128)S(1)}, f32[1,4]{1,0:T(1,128)...) fusion(f32[20,20]{1,0:T(8,128)S(1)} %multiply_select_fusion, ...), kind=kLoop, calls=%fused_computation.603 | loop fusion | flops 784 | bytes 884 | tf_op jit(solution)/shard_map/div | solution.py:61
  508.1 57.8 %fusion.191 = (f32[4]{0:T(128)S(1)}, f32[4]{0:T(128)S(1)}, f32[4]{0:T(128)S(1)}, f32[4]{0:T(128)S(1)}, f32[4]{0:T(128)S(1)}, /*index=5*/f32[4]{0:T(128)S(1)}, f3...) fusion(f32[20,20]{1,0:T(8,128)S(1)} %multiply_select_fusion, f32[1,4]{1,0:T(1,128)S(1)} %get-tuple-element.16, ...), kind=kLoop, calls=%fused_computation.505 | loop fusion | flops 704 | bytes 756 | tf_op jit(solution)/shard_map/div | solution.py:61
  565.9 19.3 %fusion.244 = (f32[1,4]{1,0:T(1,128)S(1)}, f32[4]{0:T(128)S(1)}) fusion(f32[1,4]{1,0:T(1,128)S(1)} %get-tuple-element.19, f32[1,4]{1,0:T(1,128)S(1)} %get-tuple-element.18, f32[1,4]{1,0:T(1,128)S(1)} %get-tuple-element.17, f32[1,4]{1,0:T(1,128)S(1)} %get-tuple-element.16, f32[4]{0:T(128)S(1)} %get-tuple-element.31, f32[4]{0:T(128)S(1)} %get-tuple-element.30, ...), kind=kLoop, calls=%fused_computation.657 | loop fusion | flops 240 | bytes 412 | tf_op jit(solution)/shard_map/stack | solution.py:62
  (383 shorter events, 141.4 us)
Async XLA Ops:
  0.9 15.5 %collective-permute-start.1 = (f32[4,1,32,128]{3,2,1,0:T(8,128)S(1)}, f32[4,1,32,128]{3,2,1,0:T(8,128)S(1)}, u32[]{:S(2)}, u32[]{:S(2)}) collective-permute-start(f32[4,1,32,128]{3,2,1,0:T(8,128)S(1)} %get-tuple-element.80), channel_id=1, source_target_pairs={{0,32},{32,64},{64,96},{96,128},{128,160},{160,192},{192,224},{224... | collective-permute-start | bytes 196616 | tf_op jit(solution)/shard_map/ppermute | solution.py:16
  6.5 11.0 %collective-permute-start.4 = (f32[4,1,32,128]{3,2,1,0:T(8,128)S(1)}, f32[4,1,32,128]{3,2,1,0:T(8,128)S(1)}, u32[]{:S(2)}, u32[]{:S(2)}) collective-permute-start(f32[4,1,32,128]{3,2,1,0:T(8,128)S(1)} %get-tuple-element.79), channel_id=1, source_target_pairs={{32,0},{64,32},{96,64},{128,96},{160,128},{192,160},{224,192},{256... | collective-permute-start | bytes 196616 | tf_op jit(solution)/shard_map/ppermute | solution.py:19
  12.1 8.7 %collective-permute-start.2 = (f32[4,1,32,128]{3,2,1,0:T(8,128)S(1)}, f32[4,1,32,128]{3,2,1,0:T(8,128)S(1)}, u32[]{:S(2)}, u32[]{:S(2)}) collective-permute-start(f32[4,1,32,128]{3,2,1,0:T(8,128)S(1)} %get-tuple-element.82), channel_id=1, source_target_pairs={{0,32},{32,64},{64,96},{96,128},{128,160},{160,192},{192,224},{224... | collective-permute-start | bytes 196616 | tf_op jit(solution)/shard_map/ppermute | solution.py:16
  14.0 6.8 %collective-permute-start = (f32[4,1,32,128]{3,2,1,0:T(8,128)S(1)}, f32[4,1,32,128]{3,2,1,0:T(8,128)S(1)}, u32[]{:S(2)}, u32[]{:S(2)}) collective-permute-start(f32[4,1,32,128]{3,2,1,0:T(8,128)S(1)} %get-tuple-element.81), channel_id=1, source_target_pairs={{32,0},{64,32},{96,64},{128,96},{160,128},{192,160},{224,192},{256... | collective-permute-start | bytes 196616 | tf_op jit(solution)/shard_map/ppermute | solution.py:19
  17.8 11.0 %collective-permute-start.5 = (f32[4,7,1,128]{3,1,2,0:T(8,128)S(1)}, f32[4,7,1,128]{3,1,2,0:T(8,128)S(1)}, u32[]{:S(2)}, u32[]{:S(2)}) collective-permute-start(f32[4,7,1,128]{3,1,2,0:T(8,128)S(1)} %get-tuple-element.50), channel_id=1, source_target_pairs={{0,4},{4,8},{8,12},{12,16},{16,20},{20,24},{24,28},{1,5},{5,9},{9,... | collective-permute-start | bytes 43016 | tf_op jit(solution)/shard_map/ppermute | solution.py:16
  19.4 11.3 %collective-permute-start.8 = (f32[4,7,1,128]{3,1,2,0:T(8,128)S(1)}, f32[4,7,1,128]{3,1,2,0:T(8,128)S(1)}, u32[]{:S(2)}, u32[]{:S(2)}) collective-permute-start(f32[4,7,1,128]{3,1,2,0:T(8,128)S(1)} %get-tuple-element.51), channel_id=1, source_target_pairs={{4,0},{8,4},{12,8},{16,12},{20,16},{24,20},{28,24},{5,1},{9,5},{13... | collective-permute-start | bytes 43016 | tf_op jit(solution)/shard_map/ppermute | solution.py:19
  20.9 17.0 %collective-permute-start.3 = (f32[4,7,1,128]{3,0,2,1:T(4,128)S(1)}, f32[4,7,1,128]{3,0,2,1:T(4,128)S(1)}, u32[]{:S(2)}, u32[]{:S(2)}) collective-permute-start(f32[4,7,1,128]{3,0,2,1:T(4,128)S(1)} %copy.541), channel_id=1, source_target_pairs={{4,0},{8,4},{12,8},{16,12},{20,16},{24,20},{28,24},{5,1},{9,5},{13... | collective-permute-start | bytes 43016 | tf_op jit(solution)/shard_map/ppermute | solution.py:19
  22.2 15.7 %collective-permute-start.6 = (f32[4,7,1,128]{3,0,2,1:T(4,128)S(1)}, f32[4,7,1,128]{3,0,2,1:T(4,128)S(1)}, u32[]{:S(2)}, u32[]{:S(2)}) collective-permute-start(f32[4,7,1,128]{3,0,2,1:T(4,128)S(1)} %copy.542), channel_id=1, source_target_pairs={{0,4},{4,8},{8,12},{12,16},{16,20},{20,24},{24,28},{1,5},{5,9},{9,... | collective-permute-start | bytes 43016 | tf_op jit(solution)/shard_map/ppermute | solution.py:16
  34.2 14.6 %collective-permute-start.9 = (f32[4,7,34,1]{2,1,3,0:T(8,128)}, f32[4,7,34,1]{2,1,3,0:T(8,128)}, u32[]{:S(2)}, u32[]{:S(2)}) collective-permute-start(f32[4,7,34,1]{2,1,3,0:T(8,128)} %pad_maximum_fusion.93), channel_id=1, source_target_pairs={{0,1},{1,2},{2,3},{4,5},{5,6},{6,7},{8,9},{9,10},{10,11},{12,13},{... | collective-permute-start | bytes 11432 | tf_op jit(solution)/shard_map/ppermute | solution.py:16
  40.6 10.0 %collective-permute-start.7 = (f32[4,7,34,1]{2,0,3,1:T(4,128)S(1)}, f32[4,7,34,1]{2,0,3,1:T(4,128)S(1)}, u32[]{:S(2)}, u32[]{:S(2)}) collective-permute-start(f32[4,7,34,1]{2,0,3,1:T(4,128)S(1)} %copy.469), channel_id=1, source_target_pairs={{1,0},{2,1},{3,2},{5,4},{6,5},{7,6},{9,8},{10,9},{11,10},{13,12},{... | collective-permute-start | bytes 11432 | tf_op jit(solution)/shard_map/ppermute | solution.py:19
  43.2 7.7 %collective-permute-start.10 = (f32[4,7,34,1]{2,0,3,1:T(4,128)S(1)}, f32[4,7,34,1]{2,0,3,1:T(4,128)}, u32[]{:S(2)}, u32[]{:S(2)}) collective-permute-start(f32[4,7,34,1]{2,0,3,1:T(4,128)S(1)} %copy.476), channel_id=1, source_target_pairs={{0,1},{1,2},{2,3},{4,5},{5,6},{6,7},{8,9},{9,10},{10,11},{12,13},{... | collective-permute-start | bytes 11432 | tf_op jit(solution)/shard_map/ppermute | solution.py:16
  53.9 7.3 %collective-permute-start.11 = (f32[4,1,32,128]{3,2,1,0:T(8,128)S(1)}, f32[4,1,32,128]{3,2,1,0:T(8,128)S(1)}, u32[]{:S(2)}, u32[]{:S(2)}) collective-permute-start(f32[4,1,32,128]{3,2,1,0:T(8,128)S(1)} %get-tuple-element.73), channel_id=1, source_target_pairs={{32,0},{64,32},{96,64},{128,96},{160,128},{192,160},{224,192},{256... | collective-permute-start | bytes 196616 | tf_op jit(solution)/shard_map/ppermute | solution.py:19
  55.9 6.6 %collective-permute-start.12 = (f32[4,1,32,128]{3,2,1,0:T(8,128)S(1)}, f32[4,1,32,128]{3,2,1,0:T(8,128)S(1)}, u32[]{:S(2)}, u32[]{:S(2)}) collective-permute-start(f32[4,1,32,128]{3,2,1,0:T(8,128)S(1)} %get-tuple-element.72), channel_id=1, source_target_pairs={{0,32},{32,64},{64,96},{96,128},{128,160},{160,192},{192,224},{224... | collective-permute-start | bytes 196616 | tf_op jit(solution)/shard_map/ppermute | solution.py:16
  62.6 5.6 collective-permute-start.13
  69.6 5.6 collective-permute-start.15
  78.3 8.2 %collective-permute-start.17 = (f32[4,1,32,128]{3,2,1,0:T(8,128)S(1)}, f32[4,1,32,128]{3,2,1,0:T(8,128)S(1)}, u32[]{:S(2)}, u32[]{:S(2)}) collective-permute-start(f32[4,1,32,128]{3,2,1,0:T(8,128)S(1)} %get-tuple-element.71), channel_id=1, source_target_pairs={{32,0},{64,32},{96,64},{128,96},{160,128},{192,160},{224,192},{256... | collective-permute-start | bytes 196616 | tf_op jit(solution)/shard_map/ppermute | solution.py:19
  80.3 7.6 %collective-permute-start.18 = (f32[4,1,32,128]{3,2,1,0:T(8,128)S(1)}, f32[4,1,32,128]{3,2,1,0:T(8,128)S(1)}, u32[]{:S(2)}, u32[]{:S(2)}) collective-permute-start(f32[4,1,32,128]{3,2,1,0:T(8,128)S(1)} %get-tuple-element.70), channel_id=1, source_target_pairs={{0,32},{32,64},{64,96},{96,128},{128,160},{160,192},{192,224},{224... | collective-permute-start | bytes 196616 | tf_op jit(solution)/shard_map/ppermute | solution.py:16
  87.9 5.9 collective-permute-start.19
  89.2 5.4 collective-permute-start.20
  95.2 7.0 %collective-permute-start.21 = (f32[4,7,34,1]{2,0,3,1:T(4,128)S(1)}, f32[4,7,34,1]{2,0,3,1:T(4,128)S(1)}, u32[]{:S(2)}, u32[]{:S(2)}) collective-permute-start(f32[4,7,34,1]{2,0,3,1:T(4,128)S(1)} %copy.494), channel_id=1, source_target_pairs={{1,0},{2,1},{3,2},{5,4},{6,5},{7,6},{9,8},{10,9},{11,10},{13,12},{... | collective-permute-start | bytes 11432 | tf_op jit(solution)/shard_map/ppermute | solution.py:19
  96.8 5.8 collective-permute-start.22
  105.0 8.0 %collective-permute-start.23 = (f32[4,1,32,128]{3,2,1,0:T(8,128)S(1)}, f32[4,1,32,128]{3,2,1,0:T(8,128)S(1)}, u32[]{:S(2)}, u32[]{:S(2)}) collective-permute-start(f32[4,1,32,128]{3,2,1,0:T(8,128)S(1)} %get-tuple-element.69), channel_id=1, source_target_pairs={{32,0},{64,32},{96,64},{128,96},{160,128},{192,160},{224,192},{256... | collective-permute-start | bytes 196616 | tf_op jit(solution)/shard_map/ppermute | solution.py:19
  106.9 6.9 %collective-permute-start.24 = (f32[4,1,32,128]{3,2,1,0:T(8,128)S(1)}, f32[4,1,32,128]{3,2,1,0:T(8,128)S(1)}, u32[]{:S(2)}, u32[]{:S(2)}) collective-permute-start(f32[4,1,32,128]{3,2,1,0:T(8,128)S(1)} %get-tuple-element.68), channel_id=1, source_target_pairs={{0,32},{32,64},{64,96},{96,128},{128,160},{160,192},{192,224},{224... | collective-permute-start | bytes 196616 | tf_op jit(solution)/shard_map/ppermute | solution.py:16
  113.8 6.4 %collective-permute-start.25 = (f32[4,7,1,128]{3,0,2,1:T(4,128)S(1)}, f32[4,7,1,128]{3,0,2,1:T(4,128)S(1)}, u32[]{:S(2)}, u32[]{:S(2)}) collective-permute-start(f32[4,7,1,128]{3,0,2,1:T(4,128)S(1)} %copy.498), channel_id=1, source_target_pairs={{4,0},{8,4},{12,8},{16,12},{20,16},{24,20},{28,24},{5,1},{9,5},{13... | collective-permute-start | bytes 43016 | tf_op jit(solution)/shard_map/ppermute | solution.py:19
  115.1 5.9 %collective-permute-start.26 = (f32[4,7,1,128]{3,0,2,1:T(4,128)S(1)}, f32[4,7,1,128]{3,0,2,1:T(4,128)S(1)}, u32[]{:S(2)}, u32[]{:S(2)}) collective-permute-start(f32[4,7,1,128]{3,0,2,1:T(4,128)S(1)} %copy.500), channel_id=1, source_target_pairs={{0,4},{4,8},{8,12},{12,16},{16,20},{20,24},{24,28},{1,5},{5,9},{9,... | collective-permute-start | bytes 43016 | tf_op jit(solution)/shard_map/ppermute | solution.py:16
  123.5 6.1 %collective-permute-start.27 = (f32[4,7,34,1]{2,0,3,1:T(4,128)S(1)}, f32[4,7,34,1]{2,0,3,1:T(4,128)S(1)}, u32[]{:S(2)}, u32[]{:S(2)}) collective-permute-start(f32[4,7,34,1]{2,0,3,1:T(4,128)S(1)} %copy.504), channel_id=1, source_target_pairs={{1,0},{2,1},{3,2},{5,4},{6,5},{7,6},{9,8},{10,9},{11,10},{13,12},{... | collective-permute-start | bytes 11432 | tf_op jit(solution)/shard_map/ppermute | solution.py:19
  131.3 7.9 %collective-permute-start.29 = (f32[4,1,32,128]{3,2,1,0:T(8,128)S(1)}, f32[4,1,32,128]{3,2,1,0:T(8,128)S(1)}, u32[]{:S(2)}, u32[]{:S(2)}) collective-permute-start(f32[4,1,32,128]{3,2,1,0:T(8,128)S(1)} %get-tuple-element.63), channel_id=1, source_target_pairs={{32,0},{64,32},{96,64},{128,96},{160,128},{192,160},{224,192},{256... | collective-permute-start | bytes 196616 | tf_op jit(solution)/shard_map/ppermute | solution.py:19
  133.3 7.3 %collective-permute-start.30 = (f32[4,1,32,128]{3,2,1,0:T(8,128)S(1)}, f32[4,1,32,128]{3,2,1,0:T(8,128)S(1)}, u32[]{:S(2)}, u32[]{:S(2)}) collective-permute-start(f32[4,1,32,128]{3,2,1,0:T(8,128)S(1)} %get-tuple-element.62), channel_id=1, source_target_pairs={{0,32},{32,64},{64,96},{96,128},{128,160},{160,192},{192,224},{224... | collective-permute-start | bytes 196616 | tf_op jit(solution)/shard_map/ppermute | solution.py:16
  140.6 7.6 %collective-permute-start.31 = (f32[4,7,1,128]{3,0,2,1:T(4,128)S(1)}, f32[4,7,1,128]{3,0,2,1:T(4,128)S(1)}, u32[]{:S(2)}, u32[]{:S(2)}) collective-permute-start(f32[4,7,1,128]{3,0,2,1:T(4,128)S(1)} %copy.508), channel_id=1, source_target_pairs={{4,0},{8,4},{12,8},{16,12},{20,16},{24,20},{28,24},{5,1},{9,5},{13... | collective-permute-start | bytes 43016 | tf_op jit(solution)/shard_map/ppermute | solution.py:19
  141.9 6.3 %collective-permute-start.32 = (f32[4,7,1,128]{3,0,2,1:T(4,128)S(1)}, f32[4,7,1,128]{3,0,2,1:T(4,128)S(1)}, u32[]{:S(2)}, u32[]{:S(2)}) collective-permute-start(f32[4,7,1,128]{3,0,2,1:T(4,128)S(1)} %copy.510), channel_id=1, source_target_pairs={{0,4},{4,8},{8,12},{12,16},{16,20},{20,24},{24,28},{1,5},{5,9},{9,... | collective-permute-start | bytes 43016 | tf_op jit(solution)/shard_map/ppermute | solution.py:16
  149.4 11.5 %collective-permute-start.33 = (f32[4,7,34,1]{2,0,3,1:T(4,128)}, f32[4,7,34,1]{2,0,3,1:T(4,128)}, u32[]{:S(2)}, u32[]{:S(2)}) collective-permute-start(f32[4,7,34,1]{2,0,3,1:T(4,128)} %copy.514), channel_id=1, source_target_pairs={{1,0},{2,1},{3,2},{5,4},{6,5},{7,6},{9,8},{10,9},{11,10},{13,12},{... | collective-permute-start | bytes 11432 | tf_op jit(solution)/shard_map/ppermute | solution.py:19
  151.6 10.4 %collective-permute-start.34 = (f32[4,7,34,1]{2,0,3,1:T(4,128)}, f32[4,7,34,1]{2,0,3,1:T(4,128)}, u32[]{:S(2)}, u32[]{:S(2)}) collective-permute-start(f32[4,7,34,1]{2,0,3,1:T(4,128)} %copy.516), channel_id=1, source_target_pairs={{0,1},{1,2},{2,3},{4,5},{5,6},{6,7},{8,9},{9,10},{10,11},{12,13},{... | collective-permute-start | bytes 11432 | tf_op jit(solution)/shard_map/ppermute | solution.py:16
  (35 other events, 669.8 us)
